TPU v7x, 128 devices: a whole 4x4x4 slice. The times are simulated.
128 devices in a mesh: block: 16 (over z_hi, x, core), tm: 8 (over y, z_lo).
Axes of the slice: x: 4, y: 4, z: 4 (z_hi: 2, z_lo: 2; z = z_hi * 2 + z_lo), core: 2. Of those that a mesh axis runs over, the one named last changes fastest.
Arguments:
- traces: bfloat16 [4096, 16, 6, 1024], P('block', 'tm')
- valid: int32 [4096, 16, 6], P('block', 'tm'), may hold values from 0 to 1, as said below
- panel_owner: int32 [4], replicated, may hold values from 0 to 15, as said below
- panel_start: int32 [4], replicated, may hold values from 0 to 252, as said below
Outputs:
- xcorr: float32 [16, 4096, 1024], P('tm', 'block')
Inputs may be any that keep to these rules, and one draw needn't show every extreme that they name: Within one block-tm cell (256 channels by 2 windows by 6 segments) at least an eighth of the segments are valid. `panel_owner`: the panels lie on distinct blocks. `panel_start`: multiples of 4.
All inputs are finite; a program needn't handle non-finite values.
Results may differ from a plain program's by a relative error of at most 0.0051.
Values may be sent and summed in bfloat16 or wider, within the bound.
A program may use at most 128 MiB of HBM per device.

v0:
```python
import math
import jax
import jax.numpy as jnp
from jax import lax
from jax.sharding import PartitionSpec as P

PP = 4
NP = 4


def spread(value, axis, source):
    kept = jnp.where(lax.axis_index(axis) == source, value, 0).astype(value.dtype)
    return lax.psum(kept, axis)


def forward_table(length):
    sample = jnp.arange(length, dtype=jnp.int32)
    bin_index = jnp.arange(length // 2, dtype=jnp.int32)
    angles = (sample[:, None] * bin_index[None, :] % length).astype(jnp.float32) * (
        2.0 * math.pi / length
    )
    return jnp.concatenate([jnp.cos(angles), -jnp.sin(angles)], axis=1).astype(jnp.bfloat16)


def inverse_table(length, factor):
    bin_index = jnp.arange(length // 2, dtype=jnp.int32)
    lag_index = jnp.arange(length, dtype=jnp.int32)
    angles = (bin_index[:, None] * lag_index[None, :] % length).astype(jnp.float32) * (
        2.0 * math.pi / length
    )
    weight = jnp.where(bin_index == 0, 1.0, 2.0).astype(jnp.float32)[:, None] * factor
    return jnp.concatenate([weight * jnp.cos(angles), -weight * jnp.sin(angles)], axis=0)


def whiten(segment_rows, valid_mask, forward):
    spectrum = jnp.dot(segment_rows, forward, preferred_element_type=jnp.float32)
    energy = jnp.mean(spectrum * spectrum, axis=1, keepdims=True)
    return (spectrum * lax.rsqrt(energy + 1e-06) * valid_mask[:, None].astype(jnp.float32)).astype(
        jnp.bfloat16
    )


def spectra_rows(segment_rows, valid_mask, forward):
    return whiten(segment_rows, valid_mask, forward)


def correlate(left, right):
    bins = left.shape[-1] // 2
    left_both = jnp.concatenate([left[..., :bins], left[..., bins:]], axis=1)
    right_both = jnp.concatenate([right[..., :bins], right[..., bins:]], axis=1)
    right_turn = jnp.concatenate([right[..., bins:], -right[..., :bins]], axis=1)
    real_part = jnp.einsum(
        "jmk,imk->jik", left_both, right_both, preferred_element_type=jnp.float32
    )
    imag_part = jnp.einsum(
        "jmk,imk->jik", left_both, right_turn, preferred_element_type=jnp.float32
    )
    return jnp.concatenate([real_part, imag_part], axis=-1)


def fetch_panel(whitened, panel_root, panel_first):
    candidate = lax.dynamic_slice_in_dim(whitened, panel_first, PP, 0)
    return spread(candidate, "block", panel_root)


def on_device(traces, valid, panel_owner, panel_start):
    channels, windows_here, segments, length = traces.shape
    bins = length // 2
    forward = forward_table(length)
    whitened = spectra_rows(
        traces.reshape(channels * windows_here * segments, length),
        valid.reshape(channels * windows_here * segments),
        forward,
    )
    whitened = whitened.reshape(channels, windows_here, segments, 2 * bins)
    pieces = []
    for panel in range(NP):
        pieces.append(fetch_panel(whitened, panel_owner[panel], panel_start[panel]))
    sources = jnp.concatenate(pieces, axis=0)
    groups = lax.axis_size("tm")
    inverse = inverse_table(length, 1.0 / math.sqrt(bins * windows_here * segments * groups))
    source_count = sources.shape[0]
    own_rows = whitened.reshape(channels, windows_here * segments, 2 * bins)
    source_rows = sources.reshape(source_count, windows_here * segments, 2 * bins)
    stacked = lax.psum_scatter(
        correlate(source_rows, own_rows), "tm", scatter_dimension=0, tiled=True
    )
    return jnp.dot(stacked, inverse, precision=lax.Precision.HIGHEST)


def solution(mesh):
    in_specs = (P("block", "tm", None, None), P("block", "tm", None), P(), P())
    out_specs = P("tm", "block", None)
    return jax.shard_map(
        on_device, mesh=mesh, in_specs=in_specs, out_specs=out_specs, check_vma=False
    )
```

profile of v0, /device:TPU:1, one launch (start us, length us, event | category | flops | bytes accessed | tf_op | source)
XLA Modules:
  0.0 628.7 jit_solution(12414419211468967109)
XLA Ops:
  6.5 0.0 all-reduce.3.cloned.1.call-start
  6.5 1.5 fusion.26
  13.2 8.5 %negate_convert_fusion = (bf16[1024,512]{1,0:T(8,128)(2,1)S(1)}, bf16[1024,512]{1,0:T(8,128)(2,1)S(1)}) fusion(), kind=kLoop, calls=%fused_computation.30 | loop fusion | flops 8912896 | bytes 2097152 | tf_op jit(solution)/shard_map/convert.1
  21.7 8.9 %copy.5 = bf16[256,2,6,1024]{3,2,1,0:T(8,128)(2,1)} copy(bf16[256,2,6,1024]{3,1,2,0:T(2,128)(2,1)} %param.4) | data formatting | bytes 12582912 | tf_op args[0]
  30.7 11.0 %reshape.36 = bf16[3072,1024]{1,0:T(8,128)(2,1)} reshape(bf16[256,2,6,1024]{3,2,1,0:T(8,128)(2,1)} %copy.5) | data formatting | bytes 12582912 | tf_op jit(solution)/shard_map/reshape | solution.py:71
  41.7 0.0 copy-start
  41.7 12.5 %multiply_reduce_fusion = (f32[3072]{0:T(1024)S(1)}, f32[1024,3072]{1,0:T(8,128)}) fusion(bf16[3072,1024]{1,0:T(8,128)(2,1)} %reshape.36, bf16[1024,512]{1,0:T(8,128)(2,1)S(1)} %get-tuple-element.30, bf16[1024,512]{1,0:T(8,128)(2,1)S(1)} %get-tuple-element.31), kind=kOutput, calls=%fused_computation.2 | convolution fusion | flops 6452933632 | bytes 20983808 | tf_op jit(solution)/shard_map/dot_general | solution.py:36
  54.2 0.0 copy-done
  54.2 0.2 copy.6
  54.4 0.3 convert_element_type.35
  54.7 9.0 %fusion = bf16[3072,1024]{0,1:T(8,128)(2,1)} fusion(f32[1024,3072]{1,0:T(8,128)} %get-tuple-element.29, f32[3072]{0:T(1024)S(1)} %convert_element_type.35, f32[3072]{0:T(1024)S(1)} %add_rsqrt_fusion), kind=kLoop, calls=%fused_computation.3 | loop fusion | flops 9437184 | bytes 18898944 | tf_op jit(solution)/shard_map/convert_element_type | solution.py:38
  63.7 8.6 %copy.7 = bf16[3072,1024]{1,0:T(8,128)(2,1)} copy(bf16[3072,1024]{0,1:T(8,128)(2,1)} %fusion) | data formatting | bytes 12582912 | tf_op jit(solution)/shard_map/convert_element_type | solution.py:38
  72.3 0.0 copy-start.1
  72.3 11.0 %reshape.37 = bf16[256,2,6,1024]{3,2,1,0:T(8,128)(2,1)} reshape(bf16[3072,1024]{1,0:T(8,128)(2,1)} %copy.7) | data formatting | bytes 12582912 | tf_op jit(solution)/shard_map/reshape | solution.py:75
  83.3 0.0 copy-done.1
  83.3 0.7 fusion.25
  89.0 1.9 dynamic-slice_select_fusion.3
  90.9 0.0 all-reduce.3.cloned.1.call-update
  91.0 0.2 reduce-scatter.2.cloned.1.call-start
  91.2 10.6 %reshape_reshape.3 = bf16[256,12,1024]{2,1,0:T(8,128)(2,1)} reshape(bf16[3072,1024]{1,0:T(8,128)(2,1)} %copy.7) | data formatting | bytes 12582912 | tf_op jit(solution)/shard_map/reshape;reshape | solution.py:83
  101.8 3.9 fusion.23
  105.8 7.7 %pad_maximum_fusion.1 = (bf16[256,24,512]{2,1,0:T(8,128)(2,1)}, bf16[256,24,512]{2,1,0:T(8,128)(2,1)}) fusion(bf16[256,12,512]{2,1,0:T(8,128)(2,1)S(1)} %get-tuple-element.11, bf16[256,12,512]{2,1,0:T(8,128)(2,1)S(1)} %get-tuple-element.9, bf16[256,12,512]{2,1,0:T(8,128)(2,1)S(1)} %get-tuple-element.10), kind=kLoop, calls=%fused_computation.4 | loop fusion | flops 25165824 | bytes 22020096 | tf_op jit(solution)/shard_map/concatenate | solution.py:50
  113.5 9.6 %copy.10 = bf16[256,24,512]{0,1,2:T(8,128)(2,1)} copy(bf16[256,24,512]{2,1,0:T(8,128)(2,1)} %get-tuple-element.16) | data formatting | bytes 12582912 | tf_op jit(solution)/shard_map/concatenate | solution.py:50
  123.1 9.6 %copy.13 = bf16[256,24,512]{0,1,2:T(8,128)(2,1)} copy(bf16[256,24,512]{2,1,0:T(8,128)(2,1)} %get-tuple-element.17) | data formatting | bytes 12582912 | tf_op jit(solution)/shard_map/concatenate | solution.py:51
  132.6 100.6 %all-reduce.3.cloned.1.call-done = (bf16[4,2,6,1024]{3,2,1,0:T(8,128)(2,1)}, bf16[4,2,6,1024]{3,2,1,0:T(8,128)(2,1)}, bf16[4,2,6,1024]{3,2,1,0:T(8,128)(2,1)}, bf16[4,2,6,1024]{3,2,1,0:T(8,128)(2,1)}) async-done(((bf16[4,2,6,1024]{3,2,1,0:T(8,128)(2,1)}, bf16[4,2,6,1024]{3,2,1,0:T(8,128)(2,1)}, bf16[4,2,6,1024]{3,2,1,0:T(8,128)(2,1)}, bf16[4,2,6,1024]{3,2,1,0:T(8,128)(2,1)}), ...) | async-done | bytes 393232 | tf_op jit(solution)/shard_map/psum | solution.py:13
  233.3 1.2 pad_maximum_fusion.3
  234.5 0.2 copy.9
  234.8 2.1 copy.11
  236.9 7.2 %fusion.27 = f32[512,256,16]{1,2,0:T(8,128)} fusion(bf16[256,24,512]{0,1,2:T(8,128)(2,1)} %copy.10, bf16[16,24,512]{1,0,2:T(8,128)(2,1)S(1)} %copy.11), kind=kOutput, calls=%fused_computation.53 | convolution fusion | flops 100663296 | bytes 15073280 | tf_op jit(solution)/shard_map/jmk,imk->jik/dot_general | solution.py:52
  244.2 10.0 %copy.12 = f32[512,256,16]{0,1,2:T(8,128)} copy(f32[512,256,16]{1,2,0:T(8,128)} %fusion.27) | data formatting | bytes 16777216 | tf_op jit(solution)/shard_map/jmk,imk->jik/dot_general | solution.py:52
  254.1 7.2 %fusion.28 = f32[512,256,16]{1,2,0:T(8,128)} fusion(bf16[256,24,512]{0,1,2:T(8,128)(2,1)} %copy.13, bf16[16,24,512]{1,0,2:T(8,128)(2,1)S(1)} %copy.11), kind=kOutput, calls=%fused_computation.54 | convolution fusion | flops 100663296 | bytes 15073280 | tf_op jit(solution)/shard_map/jmk,imk->jik/dot_general | solution.py:55
  261.4 10.0 %copy.14 = f32[512,256,16]{0,1,2:T(8,128)} copy(f32[512,256,16]{1,2,0:T(8,128)} %fusion.28) | data formatting | bytes 16777216 | tf_op jit(solution)/shard_map/jmk,imk->jik/dot_general | solution.py:55
  271.3 11.8 %pad_maximum_fusion = f32[16,256,1024]{2,1,0:T(8,128)} fusion(f32[16,256,512]{2,1,0:T(8,128)} %bitcast.23, f32[16,256,512]{2,1,0:T(8,128)} %bitcast.22), kind=kLoop, calls=%fused_computation | loop fusion | flops 4194304 | bytes 33554432 | tf_op jit(solution)/shard_map/concatenate | solution.py:58
  283.1 0.0 reduce-scatter.2.cloned.1.call-update
  283.1 9.2 %sine_multiply_fusion = (f32[512,1024]{1,0:T(8,128)S(1)}, f32[512,1024]{1,0:T(8,128)}) fusion(f32[512]{0:T(512)S(1)} %fusion.20, f32[512]{0:T(512)S(1)} %select_multiply_fusion), kind=kLoop, calls=%fused_computation.26 | loop fusion | flops 8388608 | bytes 4198400 | tf_op jit(solution)/shard_map/mul | solution.py:32
  292.4 318.5 %reduce-scatter.2.cloned.1.call-done = f32[2,256,1024]{2,1,0:T(8,128)} async-done(((f32[16,256,1024]{2,1,0:T(8,128)}), f32[2,256,1024]{2,1,0:T(8,128)}) %reduce-scatter.2.cloned.1.call-update) | async-done | bytes 2097168 | tf_op jit(solution)/shard_map/reduce_scatter | solution.py:85
  610.8 11.0 %fusion.1 = f32[2,256,1024]{2,1,0:T(8,128)} fusion(f32[2,256,1024]{2,1,0:T(8,128)} %reduce-scatter.2.cloned.1.call-done, f32[512,1024]{1,0:T(8,128)S(1)} %get-tuple-element.32, f32[512,1024]{1,0:T(8,128)} %get-tuple-element.33), kind=kOutput, calls=%fused_computation.7 | convolution fusion | flops 6443499520 | bytes 8388608 | tf_op jit(solution)/shard_map/dot_general | solution.py:88
  (6 shorter events, 0.1 us)
Async XLA Ops:
  6.5 226.7 %all-reduce.3.cloned.1.call-start = ((), (), s32[]{:S(2)}) async-start(), calls=%async_computation.2 | async-start | bytes 1048576 | tf_op jit(solution)/shard_map/psum | solution.py:13
  41.7 12.5 %copy-start = (s32[256,2,6]{0,1,2:T(2,128)S(1)}, s32[256,2,6]{0,1,2:T(2,128)}, u32[]{:S(2)}) copy-start(s32[256,2,6]{0,1,2:T(2,128)} %param.5) | copy-start | bytes 36868
  72.3 11.0 %copy-start.1 = (s32[4]{0:T(128)S(1)}, s32[4]{0:T(128)}, u32[]{:S(2)}) copy-start(s32[4]{0:T(128)} %param.6) | copy-start | bytes 52
  91.0 519.9 %reduce-scatter.2.cloned.1.call-start = ((), (), s32[]{:S(2)}) async-start(), calls=%async_computation.1 | async-start | bytes 18874368 | tf_op jit(solution)/shard_map/reduce_scatter | solution.py:85
Sparse Core Ops, SparseCore 0:
  91.1 142.1 all-reduce.2
  283.2 327.5 reduce-scatter.1
where the time goes:
time: 631 us; the launch traced here: 629 us
  waiting for transfers between devices  419 us (66%)
  local copies, waits for them, and re-layouts  94.3 us (15%)
  other arithmetic  53.3 us (8%)
  matrix products  37.9 us (6%)
  between operations  23.7 us (4%)
    reduce_scatter x1, waiting for transfers between devices, on_device(): lax.psum_scatter(correlate(source_rows, own_rows), 'tm', scatter_dimensio...  318 us
    psum x1, waiting for transfers between devices, spread(): return lax.psum(kept, axis)  101 us
  transfers between devices with their start and end apart: 2, of which 2 were waited for; matrix products, arithmetic and copies ran while one was open for 8% of the time, Pallas kernels for 0%

commit v1 on v0

--- a/solution.py
+++ b/solution.py
@@ -10,7 +10,7 @@
 
 def spread(value, axis, source):
     kept = jnp.where(lax.axis_index(axis) == source, value, 0).astype(value.dtype)
-    return lax.psum(kept, axis)
+    return jnp.sum(lax.all_gather(kept, axis), axis=0)
 
 
 def forward_table(length):

time: 631 us -> 686 us (1.087)
  waiting for transfers between devices: 419 us -> 460 us
    all_gather x0 -> x4, waiting for transfers between devices: none -> 144 us  [spread(): return jnp.sum(lax.all_gather(kept, axis), axis=0)]
    psum x1 -> x0, waiting for transfers between devices: 101 us -> none  [spread(): return lax.psum(kept, axis)]
    unnamed x5 -> x13, local copies, waits for them, and re-layouts: 8.95 us -> 31.2 us
    dot_general x2 -> x0, local copies, waits for them, and re-layouts: 19.9 us -> none  [the longest x1 9.96 us: correlate(): jnp.einsum('jmk,imk->jik', left_both, right_both, preferred_element_type=...]
    reduce_sum x0 -> x4, other arithmetic: none -> 11.2 us  [spread(): return jnp.sum(lax.all_gather(kept, axis), axis=0)]
    concatenate x2 -> x0, other arithmetic: 7.76 us -> none  [the longest x1 7.72 us: correlate(): right_both = jnp.concatenate([right[..., :bins], right[..., bins:]], axis=1)]
    concatenate x3 -> x1, local copies, waits for them, and re-layouts: 21.3 us -> 16.6 us  [correlate(): return jnp.concatenate([real_part, imag_part], axis=-1)]
  transfers between devices with their start and end apart: 2 -> 5, of which waited for: 2 -> 5; matrix products, arithmetic and copies ran while one was open for 8% -> 9% of each run, Pallas kernels for 0% -> 0%
where the time goes in v1:
time: 686 us; the launch traced here: 684 us
  waiting for transfers between devices  460 us (67%)
  local copies, waits for them, and re-layouts  101 us (15%)
  other arithmetic  55.8 us (8%)
  matrix products  43.5 us (6%)
  between operations  23.5 us (3%)
    reduce_scatter x1, waiting for transfers between devices, on_device(): lax.psum_scatter(correlate(source_rows, own_rows), 'tm', scatter_dimensio...  316 us
    all_gather x4, waiting for transfers between devices, spread(): return jnp.sum(lax.all_gather(kept, axis), axis=0)  144 us
    unnamed x13, local copies, waits for them, and re-layouts  31.2 us
    concatenate x1, local copies, waits for them, and re-layouts, correlate(): return jnp.concatenate([real_part, imag_part], axis=-1)  16.6 us
  transfers between devices with their start and end apart: 5, of which 5 were waited for; matrix products, arithmetic and copies ran while one was open for 9% of the time, Pallas kernels for 0%

profile of v1, /device:TPU:1, one launch (start us, length us, event | category | flops | bytes accessed | tf_op | source)
XLA Modules:
  0.0 684.1 jit_solution(18030440561483674027)
XLA Ops:
  6.5 0.0 all-gather.9.cloned.1.call-start
  6.5 1.5 fusion.42
  13.1 8.5 %negate_convert_fusion = (bf16[1024,512]{1,0:T(8,128)(2,1)S(1)}, bf16[1024,512]{1,0:T(8,128)(2,1)S(1)}) fusion(), kind=kLoop, calls=%fused_computation.39 | loop fusion | flops 8912896 | bytes 2097152 | tf_op jit(solution)/shard_map/convert.5
  21.7 9.0 %copy.47 = bf16[256,2,6,1024]{3,2,1,0:T(8,128)(2,1)} copy(bf16[256,2,6,1024]{3,1,2,0:T(2,128)(2,1)} %param.4) | data formatting | bytes 12582912 | tf_op args[0]
  30.7 11.0 %reshape.36 = bf16[3072,1024]{1,0:T(8,128)(2,1)} reshape(bf16[256,2,6,1024]{3,2,1,0:T(8,128)(2,1)} %copy.47) | data formatting | bytes 12582912 | tf_op jit(solution)/shard_map/reshape | solution.py:71
  41.7 0.0 copy-start
  41.7 12.4 %multiply_reduce_fusion = (f32[3072]{0:T(1024)S(1)}, f32[1024,3072]{1,0:T(8,128)}) fusion(bf16[3072,1024]{1,0:T(8,128)(2,1)} %reshape.36, bf16[1024,512]{1,0:T(8,128)(2,1)S(1)} %get-tuple-element.23, bf16[1024,512]{1,0:T(8,128)(2,1)S(1)} %get-tuple-element.24), kind=kOutput, calls=%fused_computation.2 | convolution fusion | flops 6452933632 | bytes 20983808 | tf_op jit(solution)/shard_map/dot_general | solution.py:36
  54.1 0.0 copy-done
  54.2 0.2 copy.48
  54.4 0.3 convert_element_type.43
  54.7 9.0 %fusion = bf16[3072,1024]{0,1:T(8,128)(2,1)} fusion(f32[1024,3072]{1,0:T(8,128)} %get-tuple-element.22, f32[3072]{0:T(1024)S(1)} %convert_element_type.43, f32[3072]{0:T(1024)S(1)} %add_rsqrt_fusion), kind=kLoop, calls=%fused_computation.3 | loop fusion | flops 9437184 | bytes 18898944 | tf_op jit(solution)/shard_map/convert_element_type | solution.py:38
  63.6 8.6 %copy.49 = bf16[3072,1024]{1,0:T(8,128)(2,1)} copy(bf16[3072,1024]{0,1:T(8,128)(2,1)} %fusion) | data formatting | bytes 12582912 | tf_op jit(solution)/shard_map/convert_element_type | solution.py:38
  72.2 0.0 copy-start.1
  72.2 11.0 %reshape.37 = bf16[256,2,6,1024]{3,2,1,0:T(8,128)(2,1)} reshape(bf16[3072,1024]{1,0:T(8,128)(2,1)} %copy.49) | data formatting | bytes 12582912 | tf_op jit(solution)/shard_map/reshape | solution.py:75
  83.2 0.0 copy-done.1
  83.2 0.7 fusion.41
  89.0 1.2 dynamic-slice_select_fusion.3
  90.2 0.7 copy.53
  90.9 0.0 all-gather.9.cloned.1.call-update
  90.9 0.0 all-gather.11.cloned.1.call-start
  91.0 0.7 copy.55
  91.7 0.0 all-gather.11.cloned.1.call-update
  91.7 0.0 all-gather.13.cloned.1.call-start
  91.8 0.7 copy.57
  92.5 0.0 all-gather.13.cloned.1.call-update
  92.6 0.2 all-gather.15.cloned.1.call-start
  92.8 0.7 copy.59
  93.5 0.0 all-gather.15.cloned.1.call-update
  93.6 0.0 reduce-scatter.2.cloned.1.call-start
  93.6 10.6 %reshape_reshape.3 = bf16[256,12,1024]{2,1,0:T(8,128)(2,1)} reshape(bf16[3072,1024]{1,0:T(8,128)(2,1)} %copy.49) | data formatting | bytes 12582912 | tf_op jit(solution)/shard_map/reshape;reshape | solution.py:83
  104.2 5.9 fusion.39
  110.2 8.5 %copy.69 = bf16[256,12,512]{0,1,2:T(8,128)(2,1)} copy(bf16[256,12,512]{2,1,0:T(8,128)(2,1)} %get-tuple-element.10) | data formatting | bytes 6291456
  118.7 8.6 %copy.70 = bf16[256,12,512]{0,1,2:T(8,128)(2,1)} copy(bf16[256,12,512]{2,1,0:T(8,128)(2,1)} %get-tuple-element.9) | data formatting | bytes 6291456
  127.3 5.0 neg.15
  132.2 9.3 %all-gather.9.cloned.1.call-done = bf16[64,2,6,1024]{3,1,2,0:T(2,128)(2,1)} async-done(((bf16[4,2,6,1024]{3,1,2,0:T(2,128)(2,1)}), bf16[64,2,6,1024]{3,1,2,0:T(2,128)(2,1)}) %all-gather.9.cloned.1.call-update) | async-done | bytes 1572880 | tf_op jit(solution)/shard_map/all_gather | solution.py:13
  141.5 2.8 reduce_sum.58
  144.4 45.1 %all-gather.11.cloned.1.call-done = bf16[64,2,6,1024]{3,1,2,0:T(2,128)(2,1)} async-done(((bf16[4,2,6,1024]{3,1,2,0:T(2,128)(2,1)}), bf16[64,2,6,1024]{3,1,2,0:T(2,128)(2,1)}) %all-gather.11.cloned.1.call-update) | async-done | bytes 1572880 | tf_op jit(solution)/shard_map/all_gather | solution.py:13
  189.4 2.8 reduce_sum.59
  192.3 45.1 %all-gather.13.cloned.1.call-done = bf16[64,2,6,1024]{3,1,2,0:T(2,128)(2,1)} async-done(((bf16[4,2,6,1024]{3,1,2,0:T(2,128)(2,1)}), bf16[64,2,6,1024]{3,1,2,0:T(2,128)(2,1)}) %all-gather.13.cloned.1.call-update) | async-done | bytes 1572880 | tf_op jit(solution)/shard_map/all_gather | solution.py:13
  237.3 2.8 reduce_sum.60
  240.2 44.9 %all-gather.15.cloned.1.call-done = bf16[64,2,6,1024]{3,1,2,0:T(2,128)(2,1)} async-done(((bf16[4,2,6,1024]{3,1,2,0:T(2,128)(2,1)}), bf16[64,2,6,1024]{3,1,2,0:T(2,128)(2,1)}) %all-gather.15.cloned.1.call-update) | async-done | bytes 1572880 | tf_op jit(solution)/shard_map/all_gather | solution.py:13
  285.1 2.8 reduce_sum.61
  287.9 0.1 pad_maximum_fusion.2
  288.1 0.2 copy.61
  288.3 2.1 copy.71
  290.5 2.9 copy.72
  293.4 10.1 %fusion.15 = f32[16,256,512]{1,0,2:T(8,128)} fusion(bf16[256,12,512]{0,1,2:T(8,128)(2,1)} %copy.70, bf16[256,12,512]{0,1,2:T(8,128)(2,1)} %copy.69, bf16[16,12,512]{1,0,2:T(8,128)(2,1)} %copy.72, bf16[16,12,512]{1,0,2:T(8,128)(2,1)S(1)} %copy.71), kind=kOutput, calls=%fused_computation.17 | convolution fusion | flops 114032640 | bytes 15073280 | tf_op jit(solution)/shard_map/jmk,imk->jik/dot_general | solution.py:52
  303.5 10.1 %fusion.12 = f32[16,256,512]{1,0,2:T(8,128)} fusion(bf16[256,12,512]{0,1,2:T(8,128)(2,1)} %neg.15, bf16[256,12,512]{0,1,2:T(8,128)(2,1)} %copy.70, bf16[16,12,512]{1,0,2:T(8,128)(2,1)} %copy.72, bf16[16,12,512]{1,0,2:T(8,128)(2,1)S(1)} %copy.71), kind=kOutput, calls=%fused_computation.16 | convolution fusion | flops 114032640 | bytes 15073280 | tf_op jit(solution)/shard_map/jmk,imk->jik/dot_general | solution.py:55
  313.5 11.6 %pad_maximum_fusion = f32[16,256,1024]{1,0,2:T(8,128)} fusion(f32[16,256,512]{1,0,2:T(8,128)} %fusion.12, f32[16,256,512]{1,0,2:T(8,128)} %fusion.15), kind=kLoop, calls=%fused_computation | loop fusion | flops 4194304 | bytes 33554432 | tf_op jit(solution)/shard_map/concatenate | solution.py:58
  325.1 16.6 %copy.64 = f32[16,256,1024]{2,1,0:T(8,128)} copy(f32[16,256,1024]{1,0,2:T(8,128)} %pad_maximum_fusion) | data formatting | bytes 33554432 | tf_op jit(solution)/shard_map/concatenate | solution.py:58
  341.7 0.0 reduce-scatter.2.cloned.1.call-update
  341.8 9.2 %sine_multiply_fusion = (f32[512,1024]{1,0:T(8,128)S(1)}, f32[512,1024]{1,0:T(8,128)}) fusion(f32[512]{0:T(512)S(1)} %fusion.34, f32[512]{0:T(512)S(1)} %select_multiply_fusion), kind=kLoop, calls=%fused_computation.35 | loop fusion | flops 8388608 | bytes 4198400 | tf_op jit(solution)/shard_map/mul | solution.py:32
  351.0 315.6 %reduce-scatter.2.cloned.1.call-done = f32[2,256,1024]{2,1,0:T(8,128)} async-done(((f32[16,256,1024]{2,1,0:T(8,128)}), f32[2,256,1024]{2,1,0:T(8,128)}) %reduce-scatter.2.cloned.1.call-update) | async-done | bytes 2097168 | tf_op jit(solution)/shard_map/reduce_scatter | solution.py:85
  666.6 11.0 %fusion.9 = f32[2,256,1024]{2,1,0:T(8,128)} fusion(f32[2,256,1024]{2,1,0:T(8,128)} %reduce-scatter.2.cloned.1.call-done, f32[512,1024]{1,0:T(8,128)S(1)} %get-tuple-element.25, f32[512,1024]{1,0:T(8,128)} %get-tuple-element.26), kind=kOutput, calls=%fused_computation.13 | convolution fusion | flops 6443499520 | bytes 8388608 | tf_op jit(solution)/shard_map/dot_general | solution.py:88
  (9 shorter events, 0.2 us)
Async XLA Ops:
  6.5 135.0 %all-gather.9.cloned.1.call-start = ((), (), s32[]{:S(2)}) async-start(), calls=%async_computation.2 | async-start | bytes 1671168 | tf_op jit(solution)/shard_map/all_gather | solution.py:13
  41.7 12.4 %copy-start = (s32[256,2,6]{0,1,2:T(2,128)S(1)}, s32[256,2,6]{0,1,2:T(2,128)}, u32[]{:S(2)}) copy-start(s32[256,2,6]{0,1,2:T(2,128)} %param.5) | copy-start | bytes 36868
  72.2 11.0 %copy-start.1 = (s32[4]{0:T(128)S(1)}, s32[4]{0:T(128)}, u32[]{:S(2)}) copy-start(s32[4]{0:T(128)} %param.6) | copy-start | bytes 52
  90.9 98.5 %all-gather.11.cloned.1.call-start = ((), (), s32[]{:S(2)}) async-start(), calls=%async_computation.3 | async-start | bytes 1671168 | tf_op jit(solution)/shard_map/all_gather | solution.py:13
  91.7 145.6 %all-gather.13.cloned.1.call-start = ((), (), s32[]{:S(2)}) async-start(), calls=%async_computation.4 | async-start | bytes 1671168 | tf_op jit(solution)/shard_map/all_gather | solution.py:13
  92.6 192.5 %all-gather.15.cloned.1.call-start = ((), (), s32[]{:S(2)}) async-start(), calls=%async_computation.5 | async-start | bytes 1671168 | tf_op jit(solution)/shard_map/all_gather | solution.py:13
  93.6 573.1 %reduce-scatter.2.cloned.1.call-start = ((), (), s32[]{:S(2)}) async-start(), calls=%async_computation.1 | async-start | bytes 18874368 | tf_op jit(solution)/shard_map/reduce_scatter | solution.py:85
Sparse Core Ops, SparseCore 0:
  91.1 50.4 all-gather.8
  144.0 45.4 all-gather.10
  191.9 45.4 all-gather.12
  239.6 45.4 all-gather.14
  341.9 324.7 reduce-scatter.1
